TPU v7x, 32 devices: a whole 2x2x4 slice. The times are simulated.
32 devices in a mesh: dp: 8 (over z, x), tensor: 4 (over y, core).
Axes of the slice: x: 2, y: 2, z: 4, core: 2. Of those that a mesh axis runs over, the one named last changes fastest.
Arguments:
- gradients: float32 [8, 16, 3, 28672], P('dp', None, None, 'tensor'), may hold values from -131072 to 131072
- token_counts: int32 [8, 3], P('dp'), may hold values from 512 to 6143
- modality: int32 [8], P('dp'), may hold values from 0 to 2
- loss_weight: float32 [3], replicated, may hold values from 0.5 to 2
- master: float32 [16, 3, 28672], P('dp', None, 'tensor'), may hold values from -6 to 6
- moment_one: float32 [16, 3, 28672], P('dp', None, 'tensor'), may hold values from -6 to 6
- moment_two: float32 [16, 3, 28672], P('dp', None, 'tensor'), may hold values from 0.05 to 2
Outputs:
- new_master: float32 [16, 3, 28672], P('dp', None, 'tensor')
- new_moment_one: float32 [16, 3, 28672], P('dp', None, 'tensor')
- new_moment_two: float32 [16, 3, 28672], P('dp', None, 'tensor')
- working_weights: bfloat16 [16, 3, 28672], P(None, None, 'tensor')
Inputs may be any that keep to these rules, and one draw needn't show every extreme that they name: `modality`: 0 is text, 1 image, 2 audio.
All inputs are finite; a program needn't handle non-finite values.
Results may differ from a plain program's by a relative error of at most 0.001.
Values may be sent and summed in bfloat16 or wider, within the bound.
A program may use at most 128 MiB of HBM per device.

v0:
```python
import jax
import jax.numpy as jnp
from jax import lax
from jax.sharding import PartitionSpec as P

beta_one = 0.9
beta_two = 0.95
bias_one = 1.0 - 0.9**10
bias_two = 1.0 - 0.95**10
epsilon = 1e-08
learn_rate = 0.01
decay_rate = 0.1


def adam_update(grad_sum, first, second, weights):
    first_new = beta_one * first + (1.0 - beta_one) * grad_sum
    second_new = beta_two * second + (1.0 - beta_two) * grad_sum * grad_sum
    step_size = first_new / bias_one / (jnp.sqrt(second_new / bias_two) + epsilon)
    weights_new = weights - learn_rate * (step_size + decay_rate * weights)
    return (weights_new, first_new, second_new)


def publish(weights_new):
    return lax.all_gather(weights_new.astype(jnp.bfloat16), "dp", axis=0, tiled=True)


def local(gradients, token_counts, modality, loss_weight, master, moment_one, moment_two):
    totals = lax.psum(token_counts[0], "dp").astype(jnp.float32)
    ratios = loss_weight / totals
    picked = (lax.iota(jnp.int32, 3) == modality[0]).astype(jnp.float32)
    own_scale = jnp.sum(picked * ratios)
    replica_grad = gradients[0]
    summed = lax.psum_scatter(replica_grad * own_scale, "dp", scatter_dimension=0, tiled=True)
    weights_new, first_new, second_new = adam_update(summed, moment_one, moment_two, master)
    return (weights_new, first_new, second_new, publish(weights_new))


def solution(mesh):
    placed = (
        P("dp", None, None, "tensor"),
        P("dp", None),
        P("dp"),
        P(),
        P("dp", None, "tensor"),
        P("dp", None, "tensor"),
        P("dp", None, "tensor"),
    )
    return jax.shard_map(
        local,
        mesh=mesh,
        in_specs=placed,
        out_specs=(
            P("dp", None, "tensor"),
            P("dp", None, "tensor"),
            P("dp", None, "tensor"),
            P(None, None, "tensor"),
        ),
        check_vma=False,
    )
```

profile of v0, /device:TPU:0, one launch (start us, length us, event | category | flops | bytes accessed | tf_op | source)
XLA Modules:
  0.0 151.2 jit_solution(16495861091149484597)
XLA Ops:
  7.2 0.0 all-reduce.3.cloned.1.call-start
  7.9 13.2 %psum.7 = s32[3]{0:T(128)S(1)} all-reduce(s32[3]{0:T(128)} %bitcast.6), channel_id=1, replica_groups=mesh['dp'=8,'tensor'=4] {'dp'}, use_global_device_ids=true, to_apply=%region_0.0 | all-reduce | flops 3 | bytes 24 | tf_op jit(solution)/shard_map/psum | solution.py:28
  21.1 1.3 fusion.1
  22.3 3.2 %multiply_bitcast_fusion = f32[16,3,7168]{2,0,1:T(8,128)} fusion(f32[1,16,3,7168]{3,1,2,0:T(8,128)} %param.7, f32[]{:T(128)} %fusion.1), kind=kLoop, calls=%fused_computation | loop fusion | flops 344064 | bytes 2752516 | tf_op jit(solution)/shard_map/mul | solution.py:33
  25.5 0.0 copy-start.3
  25.5 0.0 copy-start
  25.5 0.0 copy-start.1
  25.5 0.0 copy-start.2
  25.5 0.0 all-reduce.3.cloned.1.call-update
  25.6 0.6 copy-done.3
  26.2 0.6 dynamic-slice
  27.4 80.9 %all-reduce.3.cloned.1.call-done = f32[16,3,7168]{2,0,1:T(8,128)} async-done(((f32[16,3,7168]{2,0,1:T(8,128)}), f32[16,3,7168]{2,0,1:T(8,128)}) %all-reduce.3.cloned.1.call-update) | async-done | bytes 1376272
  108.3 0.0 copy-done
  108.3 0.0 copy-done.1
  108.3 0.0 copy-done.2
  108.3 2.5 %fusion.2 = (bf16[2,3,7168]{2,0,1:T(2,128)(2,1)S(1)}, f32[2,3,7168]{2,0,1:T(2,128)}, f32[2,3,7168]{2,0,1:T(2,128)}, f32[2,3,7168]{2,0,1:T(2,128)}) fusion(f32[2,3,7168]{2,0,1:T(2,128)S(1)} %copy-done, f32[16,3,7168]{2,0,1:T(8,128)} %all-reduce.3.cloned.1.call-done, u32[]{:T(128)S(6)} %multiply.3, f32[2,3,7168]{2,0,1:T(2,128)S(1)} %copy-done.1, ...), kind=kLoop, calls=%fused_computation.7 | loop fusion | flops 688128 | bytes 1290244 | tf_op jit(solution)/shard_map/convert_element_type | solution.py:24
  110.8 32.4 %all_gather.3 = bf16[16,3,7168]{2,1,0:T(4,128)(2,1)S(1)} all-gather(bf16[2,3,7168]{2,1,0:T(4,128)(2,1)S(1)} %copy.11), channel_id=1, replica_groups=mesh['dp'=8,'tensor'=4] {'dp'}, dimensions={0}, use_global_device_ids=true | all-gather | bytes 774144 | tf_op jit(solution)/shard_map/all_gather | solution.py:24
  143.2 1.1 copy.12
  (1 shorter events, 0.0 us)
Async XLA Ops:
  7.2 101.1 %all-reduce.3.cloned.1.call-start = ((), (), s32[]{:S(2)}) async-start(), calls=%async_computation | async-start | bytes 2752512
  25.5 0.7 copy-start.3
  25.5 82.8 %copy-start = (f32[2,3,7168]{2,0,1:T(2,128)S(1)}, f32[2,3,7168]{2,0,1:T(2,128)}, u32[]{:S(2)}) copy-start(f32[2,3,7168]{2,0,1:T(2,128)} %param.11) | copy-start | bytes 516100
  25.5 82.8 %copy-start.1 = (f32[2,3,7168]{2,0,1:T(2,128)S(1)}, f32[2,3,7168]{2,0,1:T(2,128)}, u32[]{:S(2)}) copy-start(f32[2,3,7168]{2,0,1:T(2,128)} %param.12) | copy-start | bytes 516100
  25.5 82.8 %copy-start.2 = (f32[2,3,7168]{2,0,1:T(2,128)S(1)}, f32[2,3,7168]{2,0,1:T(2,128)}, u32[]{:S(2)}) copy-start(f32[2,3,7168]{2,0,1:T(2,128)} %param.13) | copy-start | bytes 516100
Sparse Core Ops, SparseCore 0:
  25.7 82.5 all-reduce.2
where the time goes:
time: 151 us
  waiting for transfers between devices  80.9 us (54%)
  blocking collectives  45.6 us (30%)
  between operations  15.3 us (10%)
  other arithmetic  6.93 us (5%)
  local copies, waits for them, and re-layouts  2.37 us (2%)
    unnamed x2, waiting for transfers between devices  80.9 us
    all_gather x1, blocking collectives, publish(): lax.all_gather(weights_new.astype(jnp.bfloat16), 'dp', axis=0, tiled=True)  32.4 us
    psum x1, blocking collectives, local(): totals = lax.psum(token_counts[0], 'dp').astype(jnp.float32)  13.2 us
    mul x1, other arithmetic, local(): replica_grad * own_scale  3.18 us
  transfers between devices with their start and end apart: 1, of which 1 were waited for; matrix products, arithmetic and copies ran while one was open for 0% of the time, Pallas kernels for 0%

commit v1 on v0

v1 whole, which is shorter than its diff:
```python
import functools

import jax
import jax.numpy as jnp
from jax import lax
from jax.experimental import pallas as pl
from jax.experimental.pallas import tpu as pltpu
from jax.sharding import PartitionSpec as P

beta_one = 0.9
beta_two = 0.95
bias_one = 1.0 - 0.9**10
bias_two = 1.0 - 0.95**10
epsilon = 1e-08
learn_rate = 0.01
decay_rate = 0.1

WIRE = jnp.float32


def adam_update(grad_sum, first, second, weights):
    first_new = beta_one * first + (1.0 - beta_one) * grad_sum
    second_new = beta_two * second + (1.0 - beta_two) * grad_sum * grad_sum
    step_size = first_new / bias_one / (jnp.sqrt(second_new / bias_two) + epsilon)
    weights_new = weights - learn_rate * (step_size + decay_rate * weights)
    return (weights_new, first_new, second_new)


def kernel(
    n, rows_dev, mats, pieces, width,
    g_ref, counts_ref, modality_ref, weight_ref, master_ref, one_ref, two_ref,
    master_out, one_out, two_out, gathered,
    info_send, info, packed, send_a, recv_a, send_b, recv_b, own, state,
    si, ri, sa, ra, sb, rb, sc, rc, sd,
):
    half = n // 2
    me = lax.axis_index("dp")
    o, i = me // 2, me % 2
    mate = 2 * o + (1 - i)

    barrier = pltpu.get_barrier_semaphore()

    def greet(k, _):
        pl.semaphore_signal(
            barrier, inc=1, device_id={"dp": (me + k) % n}, device_id_type=pl.DeviceIdType.MESH
        )
        return 0

    lax.fori_loop(1, n, greet, 0)

    def pack(src, dst, first_row, m):
        for r in range(rows_dev):
            for p in range(pieces):
                row = r * pieces + p
                dst[row : row + 1, :] = src[pl.ds(first_row + r, 1), m, p * width : (p + 1) * width]

    def remote(src, dst, send, recv, target):
        return pltpu.make_async_remote_copy(
            src_ref=src,
            dst_ref=dst,
            send_sem=send,
            recv_sem=recv,
            device_id={"dp": target},
            device_id_type=pl.DeviceIdType.MESH,
        )

    g = g_ref.at[0]

    line = lax.broadcasted_iota(jnp.int32, info_send.shape, 0)
    told = jnp.where(line == 3, modality_ref[0], 0)
    for m in range(3):
        told = jnp.where(line == m, counts_ref[0, m], told)
    info_send[...] = told
    info[me] = told

    def copy_a(od, m):
        return remote(send_a.at[od, m], recv_a.at[od, m], sa.at[od, m], ra.at[od, m], mate)

    def fill_a(k, m):
        od = (o + 1 + k) % half
        d = 2 * od + (1 - i)
        pack(g, packed.at[d, m], d * rows_dev, m)
        send_a[od, m] = packed[d, m]

    fill_a(0, 0)
    pl.semaphore_wait(barrier, n - 1)
    copy_a((o + 1) % half, 0).start()

    def tell(k, _):
        remote(info_send, info.at[me], si.at[k], ri.at[me], (me + k) % n).start()
        return 0

    lax.fori_loop(1, n, tell, 0)

    for m in range(mats):
        def step_a(k, _, m=m):
            fill_a(k, m)
            copy_a((o + 1 + k) % half, m).start()
            return 0

        lax.fori_loop(1 if m == 0 else 0, half, step_a, 0)

    for m in range(mats):
        def keep(od, _, m=m):
            d = 2 * od + i
            pack(g, packed.at[d, m], d * rows_dev, m)
            return 0

        lax.fori_loop(0, half, keep, 0)

    def hear(k, _):
        source = (me + k) % n
        remote(info_send, info.at[source], si.at[k], ri.at[source], source).wait()
        return 0

    lax.fori_loop(1, n, hear, 0)

    totals = lax.fori_loop(1, n, lambda r, t: t + info[r], info[0])
    ratios = [weight_ref[m] / totals[m : m + 1].astype(jnp.float32) for m in range(3)]

    def scale_of(replica):
        kind = info[replica][3:4]
        picked = jnp.where(kind == 2, ratios[2], jnp.where(kind == 1, ratios[1], ratios[0]))
        return jnp.concatenate([picked] * (width // 128), axis=1)

    my_scale = scale_of(me)
    mate_scale = scale_of(mate)

    def copy_b(od, m):
        return remote(send_b.at[od, m], recv_b.at[o, m], sb.at[od, m], rb.at[o, m], 2 * od + i)

    def paired(od, m):
        copy_a(od, m).wait()
        return packed[2 * od + i, m] * my_scale + recv_a[od, m] * mate_scale

    def phase_b(m):
        def step(k, _):
            od = (o + 1 + k) % half
            send_b[od, m] = paired(od, m)
            copy_b(od, m).start()
            return 0

        lax.fori_loop(0, half - 1, step, 0)
        own[m] = paired(o, m)

    def copy_c(target, slot, m):
        return remote(gathered.at[me, m], gathered.at[me, m], sc.at[slot, m], rc.at[me, m], target)

    def finish(m):
        pack(master_ref, state.at[0, m], 0, m)
        pack(one_ref, state.at[1, m], 0, m)
        pack(two_ref, state.at[2, m], 0, m)

        def add(k, total):
            source = (o + k) % half
            pltpu.make_async_remote_copy(
                src_ref=send_b.at[source, m], dst_ref=recv_b.at[source, m],
                send_sem=sb.at[source, m], recv_sem=rb.at[source, m],
                device_id={"dp": mate}, device_id_type=pl.DeviceIdType.MESH,
            ).wait()
            return total + recv_b[source, m]

        summed = lax.fori_loop(1, half, add, own[m])
        weights_new, first_new, second_new = adam_update(summed, state[1, m], state[2, m], state[0, m])
        gathered[me, m] = weights_new.astype(jnp.bfloat16)
        copy_c(mate, 0, m).start()

        def spread(k, _):
            copy_c(2 * ((o + k) % half) + i, k, m).start()
            return 0

        lax.fori_loop(1, half, spread, 0)
        state[0, m] = weights_new
        state[1, m] = first_new
        state[2, m] = second_new
        for slot, out in enumerate((master_out, one_out, two_out)):
            for r in range(rows_dev):
                for p in range(pieces):
                    row = r * pieces + p
                    out[r : r + 1, m, p * width : (p + 1) * width] = state[slot, m, row : row + 1, :]

    def copy_d(od, m):
        d = 2 * od + i
        return remote(gathered.at[d, m], gathered.at[d, m], sd.at[od, m], rc.at[d, m], mate)

    def forward(m):
        def step(k, _):
            od = (o + k) % half
            d = 2 * od + i
            remote(gathered.at[d, m], gathered.at[d, m], sd.at[od, m], rc.at[d, m], mate).wait_recv()
            copy_d(od, m).start()
            return 0

        lax.fori_loop(1, half, step, 0)

    phase_b(0)
    for m in range(mats):
        if m + 1 < mats:
            phase_b(m + 1)
        finish(m)
        if m > 0:
            forward(m - 1)
    forward(mats - 1)

    for m in range(mats):
        def last(k, _, m=m):
            od = (o + k) % half
            copy_c(mate, k, m).wait_send()
            d = 2 * od + (1 - i)
            remote(gathered.at[d, m], gathered.at[d, m], sd.at[od, m], rc.at[d, m], mate).wait_recv()
            return 0

        lax.fori_loop(0, half, last, 0)

        def sent(k, _, m=m):
            copy_d((o + k) % half, m).wait_send()
            return 0

        lax.fori_loop(1, half, sent, 0)


def local(n, gradients, token_counts, modality, loss_weight, master, moment_one, moment_two):
    rows_dev, mats, columns = master.shape
    half = n // 2
    pieces = 8
    width = columns // pieces
    lines = rows_dev * pieces
    vmem = pl.BlockSpec(memory_space=pltpu.VMEM)
    smem = pl.BlockSpec(memory_space=pltpu.SMEM)
    dma = pltpu.SemaphoreType.DMA
    state_shape = jax.ShapeDtypeStruct(master.shape, jnp.float32)
    weights_new, first_new, second_new, gathered = pl.pallas_call(
        functools.partial(kernel, n, rows_dev, mats, pieces, width),
        out_shape=(
            state_shape,
            state_shape,
            state_shape,
            jax.ShapeDtypeStruct((n, mats, lines, width), jnp.bfloat16),
        ),
        in_specs=[vmem, smem, smem, smem, vmem, vmem, vmem],
        out_specs=(vmem,) * 4,
        scratch_shapes=[
            pltpu.VMEM((8, 128), jnp.int32),
            pltpu.VMEM((n, 8, 128), jnp.int32),
            pltpu.VMEM((n, mats, lines, width), jnp.float32),
            pltpu.VMEM((half, mats, lines, width), WIRE),
            pltpu.VMEM((half, mats, lines, width), WIRE),
            pltpu.VMEM((half, mats, lines, width), WIRE),
            pltpu.VMEM((half, mats, lines, width), WIRE),
            pltpu.VMEM((mats, lines, width), jnp.float32),
            pltpu.VMEM((3, mats, lines, width), jnp.float32),
            dma((n,)),
            dma((n,)),
            dma((half, mats)),
            dma((half, mats)),
            dma((half, mats)),
            dma((half, mats)),
            dma((half, mats)),
            dma((n, mats)),
            dma((half, mats)),
        ],
        compiler_params=pltpu.CompilerParams(
            collective_id=0, has_side_effects=True, vmem_limit_bytes=60 * 2**20
        ),
    )(gradients, token_counts, modality, loss_weight, master, moment_one, moment_two)
    working = gathered.reshape(n, mats, rows_dev, columns).transpose(0, 2, 1, 3)
    return (weights_new, first_new, second_new, working.reshape(n * rows_dev, mats, columns))


def solution(mesh):
    placed = (
        P("dp", None, None, "tensor"),
        P("dp", None),
        P("dp"),
        P(),
        P("dp", None, "tensor"),
        P("dp", None, "tensor"),
        P("dp", None, "tensor"),
    )
    return jax.shard_map(
        functools.partial(local, mesh.shape["dp"]),
        mesh=mesh,
        in_specs=placed,
        out_specs=(
            P("dp", None, "tensor"),
            P("dp", None, "tensor"),
            P("dp", None, "tensor"),
            P(None, None, "tensor"),
        ),
        check_vma=False,
    )
```

time: 151 us -> 59.7 us (0.40)
  waiting for transfers between devices: 80.9 us -> 0 us
  blocking collectives: 45.6 us -> 0 us
  Pallas kernels: 0 us -> 40.7 us
  local copies, waits for them, and re-layouts: 2.37 us -> 17.4 us
  between operations: 15.3 us -> 1.3 us
  other arithmetic: 6.93 us -> 0 us
    unnamed x2 -> x0, waiting for transfers between devices: 80.9 us -> none
    pallas_call x0 -> x1, Pallas kernels: none -> 40.7 us  [local(): pl.pallas_call(functools.partial(kernel, n, rows_dev, mats, pieces, width...]
    all_gather x1 -> x0, blocking collectives: 32.4 us -> none  [publish(): lax.all_gather(weights_new.astype(jnp.bfloat16), 'dp', axis=0, tiled=True)]
    psum x1 -> x0, blocking collectives: 13.2 us -> none  [local(): totals = lax.psum(token_counts[0], 'dp').astype(jnp.float32)]
    unnamed x10 -> x7, local copies, waits for them, and re-layouts: 2.33 us -> 13.9 us
    mul x1 -> x0, other arithmetic: 3.18 us -> none  [local(): replica_grad * own_scale]
    reshape x0 -> x2, local copies, waits for them, and re-layouts: none -> 3.03 us  [the longest x1 1.93 us: local(): working = gathered.reshape(n, mats, rows_dev, columns).transpose(0, 2, 1, 3)]
    convert_element_type x1 -> x0, other arithmetic: 2.48 us -> none  [publish(): weights_new.astype(jnp.bfloat16)]
  transfers between devices with their start and end apart: 1 -> 0, of which waited for: 1 -> 0; matrix products, arithmetic and copies ran while one was open for 0% -> 0% of each run, Pallas kernels for 0% -> 0%
where the time goes in v1:
time: 59.7 us; the launch traced here: 59.4 us
  Pallas kernels  40.7 us (68%)
  local copies, waits for them, and re-layouts  17.4 us (29%)
  between operations  1.3 us (2%)
    pallas_call x1, Pallas kernels, local(): pl.pallas_call(functools.partial(kernel, n, rows_dev, mats, pieces, width...  40.7 us
    unnamed x7, local copies, waits for them, and re-layouts  13.9 us
    reshape x1, local copies, waits for them, and re-layouts, local(): working = gathered.reshape(n, mats, rows_dev, columns).transpose(0, 2, 1, 3)  1.93 us

profile of v1, /device:TPU:0, one launch (start us, length us, event | category | flops | bytes accessed | tf_op | source)
XLA Modules:
  0.0 59.4 jit_solution(5779384223788265295)
XLA Ops:
  1.3 1.7 %copy.12.master_ref = f32[2,3,7168]{2,1,0:T(4,128)} copy(f32[2,3,7168]{2,0,1:T(2,128)} %param.11) | data formatting | bytes 344064 | tf_op args[4]
  3.0 1.7 %copy.13.one_ref = f32[2,3,7168]{2,1,0:T(4,128)} copy(f32[2,3,7168]{2,0,1:T(2,128)} %param.12) | data formatting | bytes 344064 | tf_op args[5]
  4.7 1.7 %copy.14.two_ref = f32[2,3,7168]{2,1,0:T(4,128)} copy(f32[2,3,7168]{2,0,1:T(2,128)} %param.13) | data formatting | bytes 344064 | tf_op args[6]
  6.4 3.5 %copy.11.g_ref = f32[1,16,3,7168]{3,2,1,0:T(4,128)} copy(f32[1,16,3,7168]{3,1,2,0:T(8,128)} %param.7) | data formatting | bytes 2752512 | tf_op args[0]
  9.9 40.7 %shard_map.102 = (f32[2,3,7168]{2,1,0:T(4,128)}, f32[2,3,7168]{2,1,0:T(4,128)}, f32[2,3,7168]{2,1,0:T(4,128)}, bf16[8,3,16,896]{3,2,1,0:T(8,128)(2,1)}) custom-call(f32[1,16,3,7168]{3,2,1,0:T(4,128)} %copy.11.g_ref, s32[1,3]{1,0:T(1,128)} %counts_ref.1, s32[1]{0:T(128)S(6)} %copy.19.modality_ref, f32[3]{0:T(128)} %weight_ref.1, ...), custom_call_target="tpu_custom_call" | custom-call | tf_op jit(solution)/shard_map/pallas_call | solution.py:232
  50.6 1.7 %copy.16 = f32[2,3,7168]{2,0,1:T(2,128)} copy(f32[2,3,7168]{2,1,0:T(4,128)} %get-tuple-element.12) | data formatting | bytes 344064
  52.4 1.7 %copy.17 = f32[2,3,7168]{2,0,1:T(2,128)} copy(f32[2,3,7168]{2,1,0:T(4,128)} %get-tuple-element.13) | data formatting | bytes 344064
  54.1 1.7 %copy.18 = f32[2,3,7168]{2,0,1:T(2,128)} copy(f32[2,3,7168]{2,1,0:T(4,128)} %get-tuple-element.14) | data formatting | bytes 344064
  55.8 1.9 %reshape.14 = bf16[8,3,2,7168]{3,2,1,0:T(2,128)(2,1)S(1)} reshape(bf16[8,3,16,896]{3,2,1,0:T(8,128)(2,1)} %get-tuple-element.11) | data formatting | bytes 1376256 | tf_op jit(solution)/shard_map/reshape | solution.py:266
  57.8 0.5 copy.15
  58.3 1.1 %reshape.15 = bf16[16,3,7168]{2,0,1:T(8,128)(2,1)} reshape(bf16[8,2,3,7168]{3,1,0,2:T(2,128)(2,1)S(1)} %copy.15) | data formatting | bytes 1376256 | tf_op jit(solution)/shard_map/reshape | solution.py:267

commit v2 on v1

--- a/solution.py
+++ b/solution.py
@@ -29,8 +29,8 @@
 def kernel(
     n, rows_dev, mats, pieces, width,
     g_ref, counts_ref, modality_ref, weight_ref, master_ref, one_ref, two_ref,
-    master_out, one_out, two_out, gathered,
-    info_send, info, packed, send_a, recv_a, send_b, recv_b, own, state,
+    master_out, one_out, two_out, working,
+    info_send, info, gathered, spread_out, kept, send_a, recv_a, send_b, recv_b, own, state,
     si, ri, sa, ra, sb, rb, sc, rc, sd,
 ):
     half = n // 2
@@ -52,7 +52,7 @@
         for r in range(rows_dev):
             for p in range(pieces):
                 row = r * pieces + p
-                dst[row : row + 1, :] = src[pl.ds(first_row + r, 1), m, p * width : (p + 1) * width]
+                dst[row : row + 1, :] = src[m, pl.ds(first_row + r, 1), p * width : (p + 1) * width]
 
     def remote(src, dst, send, recv, target):
         return pltpu.make_async_remote_copy(
@@ -79,8 +79,7 @@
     def fill_a(k, m):
         od = (o + 1 + k) % half
         d = 2 * od + (1 - i)
-        pack(g, packed.at[d, m], d * rows_dev, m)
-        send_a[od, m] = packed[d, m]
+        pack(g, send_a.at[od, m], d * rows_dev, m)
 
     fill_a(0, 0)
     pl.semaphore_wait(barrier, n - 1)
@@ -102,8 +101,7 @@
 
     for m in range(mats):
         def keep(od, _, m=m):
-            d = 2 * od + i
-            pack(g, packed.at[d, m], d * rows_dev, m)
+            pack(g, kept.at[od, m], (2 * od + i) * rows_dev, m)
             return 0
 
         lax.fori_loop(0, half, keep, 0)
@@ -131,7 +129,7 @@
 
     def paired(od, m):
         copy_a(od, m).wait()
-        return packed[2 * od + i, m] * my_scale + recv_a[od, m] * mate_scale
+        return kept[od, m] * my_scale + recv_a[od, m] * mate_scale
 
     def phase_b(m):
         def step(k, _):
@@ -177,7 +175,7 @@
             for r in range(rows_dev):
                 for p in range(pieces):
                     row = r * pieces + p
-                    out[r : r + 1, m, p * width : (p + 1) * width] = state[slot, m, row : row + 1, :]
+                    out[m, r : r + 1, p * width : (p + 1) * width] = state[slot, m, row : row + 1, :]
 
     def copy_d(od, m):
         d = 2 * od + i
@@ -193,6 +191,13 @@
 
         lax.fori_loop(1, half, step, 0)
 
+    def unpack(d, m):
+        block = gathered[d, m].astype(jnp.float32)
+        for r in range(rows_dev):
+            for p in range(pieces):
+                row = r * pieces + p
+                spread_out[pl.ds(d * rows_dev + r, 1), p * width : (p + 1) * width] = block[row : row + 1, :]
+
     phase_b(0)
     for m in range(mats):
         if m + 1 < mats:
@@ -203,14 +208,28 @@
     forward(mats - 1)
 
     for m in range(mats):
+        def held(od, _, m=m):
+            unpack(2 * od + i, m)
+            return 0
+
+        lax.fori_loop(0, half, held, 0)
+
         def last(k, _, m=m):
             od = (o + k) % half
-            copy_c(mate, k, m).wait_send()
             d = 2 * od + (1 - i)
             remote(gathered.at[d, m], gathered.at[d, m], sd.at[od, m], rc.at[d, m], mate).wait_recv()
+            unpack(d, m)
             return 0
 
         lax.fori_loop(0, half, last, 0)
+        working[m] = spread_out[...].astype(jnp.bfloat16)
+
+    for m in range(mats):
+        def given(k, _, m=m):
+            copy_c(mate, k, m).wait_send()
+            return 0
+
+        lax.fori_loop(0, half, given, 0)
 
         def sent(k, _, m=m):
             copy_d((o + k) % half, m).wait_send()
@@ -228,21 +247,23 @@
     vmem = pl.BlockSpec(memory_space=pltpu.VMEM)
     smem = pl.BlockSpec(memory_space=pltpu.SMEM)
     dma = pltpu.SemaphoreType.DMA
-    state_shape = jax.ShapeDtypeStruct(master.shape, jnp.float32)
-    weights_new, first_new, second_new, gathered = pl.pallas_call(
+    state_shape = jax.ShapeDtypeStruct((mats, rows_dev, columns), jnp.float32)
+    weights_new, first_new, second_new, working = pl.pallas_call(
         functools.partial(kernel, n, rows_dev, mats, pieces, width),
         out_shape=(
             state_shape,
             state_shape,
             state_shape,
-            jax.ShapeDtypeStruct((n, mats, lines, width), jnp.bfloat16),
+            jax.ShapeDtypeStruct((mats, n * rows_dev, columns), jnp.bfloat16),
         ),
         in_specs=[vmem, smem, smem, smem, vmem, vmem, vmem],
         out_specs=(vmem,) * 4,
         scratch_shapes=[
             pltpu.VMEM((8, 128), jnp.int32),
             pltpu.VMEM((n, 8, 128), jnp.int32),
-            pltpu.VMEM((n, mats, lines, width), jnp.float32),
+            pltpu.VMEM((n, mats, lines, width), jnp.bfloat16),
+            pltpu.VMEM((n * rows_dev, columns), jnp.float32),
+            pltpu.VMEM((half, mats, lines, width), jnp.float32),
             pltpu.VMEM((half, mats, lines, width), WIRE),
             pltpu.VMEM((half, mats, lines, width), WIRE),
             pltpu.VMEM((half, mats, lines, width), WIRE),
@@ -262,9 +283,11 @@
         compiler_params=pltpu.CompilerParams(
             collective_id=0, has_side_effects=True, vmem_limit_bytes=60 * 2**20
         ),
-    )(gradients, token_counts, modality, loss_weight, master, moment_one, moment_two)
-    working = gathered.reshape(n, mats, rows_dev, columns).transpose(0, 2, 1, 3)
-    return (weights_new, first_new, second_new, working.reshape(n * rows_dev, mats, columns))
+    )(
+        gradients.transpose(0, 2, 1, 3), token_counts, modality, loss_weight,
+        master.transpose(1, 0, 2), moment_one.transpose(1, 0, 2), moment_two.transpose(1, 0, 2),
+    )
+    return tuple(a.transpose(1, 0, 2) for a in (weights_new, first_new, second_new, working))
 
 
 def solution(mesh):

time: 59.7 us -> 47.9 us (0.80)
  local copies, waits for them, and re-layouts: 17.4 us -> 5.71 us
    unnamed x7 -> x6, local copies, waits for them, and re-layouts: 13.9 us -> 5.71 us
    reshape x2 -> x0, local copies, waits for them, and re-layouts: 3.03 us -> none  [the longest x1 1.93 us: local(): working = gathered.reshape(n, mats, rows_dev, columns).transpose(0, 2, 1, 3)]
where the time goes in v2:
time: 47.9 us; the launch traced here: 47.7 us
  Pallas kernels  40.7 us (85%)
  local copies, waits for them, and re-layouts  5.71 us (12%)
  between operations  1.3 us (3%)
    pallas_call x1, Pallas kernels, local(): pl.pallas_call(functools.partial(kernel, n, rows_dev, mats, pieces, width...  40.7 us
    unnamed x6, local copies, waits for them, and re-layouts  5.71 us

profile of v2, /device:TPU:0, one launch (start us, length us, event | category | flops | bytes accessed | tf_op | source)
XLA Modules:
  0.0 47.7 jit_solution(13098058028457055411)
XLA Ops:
  1.3 40.7 %shard_map.102 = (f32[3,2,7168]{2,1,0:T(2,128)}, f32[3,2,7168]{2,1,0:T(2,128)}, f32[3,2,7168]{2,1,0:T(2,128)}, bf16[3,16,7168]{2,1,0:T(8,128)(2,1)}) custom-call(f32[1,3,16,7168]{3,2,1,0:T(8,128)} %bitcast.8, s32[1,3]{1,0:T(1,128)} %counts_ref.1, s32[1]{0:T(128)S(6)} %copy.15.modality_ref, f32[3]{0:T(128)} %weight_ref.1, f32[3,2,7168]{2,1,0:T(2,128)} %bitcast.13, ...), custom_call_target="tpu_custom_call" | custom-call | tf_op jit(solution)/shard_map/pallas_call | solution.py:251
  42.0 0.0 copy-start
  42.0 1.7 %copy.16 = f32[2,3,7168]{2,0,1:T(2,128)} copy(f32[2,3,7168]{2,0,1:T(2,128)} %bitcast.12) | data formatting | bytes 344064
  43.7 1.6 %copy.17 = f32[2,3,7168]{2,0,1:T(2,128)} copy(f32[2,3,7168]{2,0,1:T(2,128)} %bitcast.11) | data formatting | bytes 344064
  45.3 1.6 %copy.18 = f32[2,3,7168]{2,0,1:T(2,128)} copy(f32[2,3,7168]{2,0,1:T(2,128)} %bitcast.10) | data formatting | bytes 344064
  46.9 0.0 copy-done
  46.9 0.8 %copy.19 = bf16[16,3,7168]{2,0,1:T(8,128)(2,1)} copy(bf16[16,3,7168]{2,0,1:T(8,128)(2,1)S(1)} %bitcast.9) | data formatting | bytes 1376256
Async XLA Ops:
  42.0 4.9 %copy-start = (bf16[3,16,7168]{2,1,0:T(8,128)(2,1)S(1)}, bf16[3,16,7168]{2,1,0:T(8,128)(2,1)}, u32[]{:S(2)}) copy-start(bf16[3,16,7168]{2,1,0:T(8,128)(2,1)} %get-tuple-element.11) | copy-start | bytes 2064388

commit v3 on v2

--- a/solution.py
+++ b/solution.py
@@ -48,11 +48,19 @@
 
     lax.fori_loop(1, n, greet, 0)
 
-    def pack(src, dst, first_row, m):
+    cut = (width // 128 + 1) // 2 * 128
+    chunks = [(m, lo, hi) for m in range(mats) for lo, hi in ((0, cut), (cut, width))]
+
+    def part(ref, index, c):
+        m, lo, hi = chunks[c]
+        return ref.at[index, m, :, lo:hi]
+
+    def pack(src, dst, first_row, c):
+        m, lo, hi = chunks[c]
         for r in range(rows_dev):
             for p in range(pieces):
                 row = r * pieces + p
-                dst[row : row + 1, :] = src[m, pl.ds(first_row + r, 1), p * width : (p + 1) * width]
+                dst[row : row + 1, lo:hi] = src[m, pl.ds(first_row + r, 1), p * width + lo : p * width + hi]
 
     def remote(src, dst, send, recv, target):
         return pltpu.make_async_remote_copy(
@@ -74,12 +82,12 @@
     info[me] = told
 
     def copy_a(od, m):
-        return remote(send_a.at[od, m], recv_a.at[od, m], sa.at[od, m], ra.at[od, m], mate)
+        return remote(part(send_a, od, m), part(recv_a, od, m), sa.at[od, m], ra.at[od, m], mate)
 
     def fill_a(k, m):
         od = (o + 1 + k) % half
         d = 2 * od + (1 - i)
-        pack(g, send_a.at[od, m], d * rows_dev, m)
+        pack(g, send_a.at[od, chunks[m][0]], d * rows_dev, m)
 
     fill_a(0, 0)
     pl.semaphore_wait(barrier, n - 1)
@@ -91,7 +99,7 @@
 
     lax.fori_loop(1, n, tell, 0)
 
-    for m in range(mats):
+    for m in range(len(chunks)):
         def step_a(k, _, m=m):
             fill_a(k, m)
             copy_a((o + 1 + k) % half, m).start()
@@ -99,9 +107,9 @@
 
         lax.fori_loop(1 if m == 0 else 0, half, step_a, 0)
 
-    for m in range(mats):
+    for m in range(len(chunks)):
         def keep(od, _, m=m):
-            pack(g, kept.at[od, m], (2 * od + i) * rows_dev, m)
+            pack(g, kept.at[od, chunks[m][0]], (2 * od + i) * rows_dev, m)
             return 0
 
         lax.fori_loop(0, half, keep, 0)
@@ -125,42 +133,47 @@
     mate_scale = scale_of(mate)
 
     def copy_b(od, m):
-        return remote(send_b.at[od, m], recv_b.at[o, m], sb.at[od, m], rb.at[o, m], 2 * od + i)
+        return remote(part(send_b, od, m), part(recv_b, o, m), sb.at[od, m], rb.at[o, m], 2 * od + i)
 
     def paired(od, m):
         copy_a(od, m).wait()
-        return kept[od, m] * my_scale + recv_a[od, m] * mate_scale
+        mat, lo, hi = chunks[m]
+        mine = kept[od, mat, :, lo:hi] * my_scale[:, lo:hi]
+        return mine + recv_a[od, mat, :, lo:hi] * mate_scale[:, lo:hi]
 
     def phase_b(m):
+        mat, lo, hi = chunks[m]
+
         def step(k, _):
             od = (o + 1 + k) % half
-            send_b[od, m] = paired(od, m)
+            send_b[od, mat, :, lo:hi] = paired(od, m)
             copy_b(od, m).start()
             return 0
 
         lax.fori_loop(0, half - 1, step, 0)
-        own[m] = paired(o, m)
+        own[mat, :, lo:hi] = paired(o, m)
 
     def copy_c(target, slot, m):
-        return remote(gathered.at[me, m], gathered.at[me, m], sc.at[slot, m], rc.at[me, m], target)
+        return remote(part(gathered, me, m), part(gathered, me, m), sc.at[slot, m], rc.at[me, m], target)
 
     def finish(m):
-        pack(master_ref, state.at[0, m], 0, m)
-        pack(one_ref, state.at[1, m], 0, m)
-        pack(two_ref, state.at[2, m], 0, m)
+        mat, lo, hi = chunks[m]
+        pack(master_ref, state.at[0, chunks[m][0]], 0, m)
+        pack(one_ref, state.at[1, chunks[m][0]], 0, m)
+        pack(two_ref, state.at[2, chunks[m][0]], 0, m)
 
         def add(k, total):
             source = (o + k) % half
             pltpu.make_async_remote_copy(
-                src_ref=send_b.at[source, m], dst_ref=recv_b.at[source, m],
+                src_ref=part(send_b, source, m), dst_ref=part(recv_b, source, m),
                 send_sem=sb.at[source, m], recv_sem=rb.at[source, m],
                 device_id={"dp": mate}, device_id_type=pl.DeviceIdType.MESH,
             ).wait()
-            return total + recv_b[source, m]
-
-        summed = lax.fori_loop(1, half, add, own[m])
-        weights_new, first_new, second_new = adam_update(summed, state[1, m], state[2, m], state[0, m])
-        gathered[me, m] = weights_new.astype(jnp.bfloat16)
+            return total + recv_b[source, mat, :, lo:hi]
+
+        summed = lax.fori_loop(1, half, add, own[mat, :, lo:hi])
+        weights_new, first_new, second_new = adam_update(summed, state[1, mat, :, lo:hi], state[2, mat, :, lo:hi], state[0, mat, :, lo:hi])
+        gathered[me, mat, :, lo:hi] = weights_new.astype(jnp.bfloat16)
         copy_c(mate, 0, m).start()
 
         def spread(k, _):
@@ -168,46 +181,47 @@
             return 0
 
         lax.fori_loop(1, half, spread, 0)
-        state[0, m] = weights_new
-        state[1, m] = first_new
-        state[2, m] = second_new
+        state[0, mat, :, lo:hi] = weights_new
+        state[1, mat, :, lo:hi] = first_new
+        state[2, mat, :, lo:hi] = second_new
         for slot, out in enumerate((master_out, one_out, two_out)):
             for r in range(rows_dev):
                 for p in range(pieces):
                     row = r * pieces + p
-                    out[m, r : r + 1, p * width : (p + 1) * width] = state[slot, m, row : row + 1, :]
+                    out[mat, r : r + 1, p * width + lo : p * width + hi] = state[slot, mat, row : row + 1, lo:hi]
 
     def copy_d(od, m):
         d = 2 * od + i
-        return remote(gathered.at[d, m], gathered.at[d, m], sd.at[od, m], rc.at[d, m], mate)
+        return remote(part(gathered, d, m), part(gathered, d, m), sd.at[od, m], rc.at[d, m], mate)
 
     def forward(m):
         def step(k, _):
             od = (o + k) % half
             d = 2 * od + i
-            remote(gathered.at[d, m], gathered.at[d, m], sd.at[od, m], rc.at[d, m], mate).wait_recv()
+            remote(part(gathered, d, m), part(gathered, d, m), sd.at[od, m], rc.at[d, m], mate).wait_recv()
             copy_d(od, m).start()
             return 0
 
         lax.fori_loop(1, half, step, 0)
 
     def unpack(d, m):
-        block = gathered[d, m].astype(jnp.float32)
+        mat, lo, hi = chunks[m]
+        block = gathered[d, mat, :, lo:hi].astype(jnp.float32)
         for r in range(rows_dev):
             for p in range(pieces):
                 row = r * pieces + p
-                spread_out[pl.ds(d * rows_dev + r, 1), p * width : (p + 1) * width] = block[row : row + 1, :]
+                spread_out[pl.ds(d * rows_dev + r, 1), p * width + lo : p * width + hi] = block[row : row + 1, :]
 
     phase_b(0)
-    for m in range(mats):
-        if m + 1 < mats:
+    for m in range(len(chunks)):
+        if m + 1 < len(chunks):
             phase_b(m + 1)
         finish(m)
         if m > 0:
             forward(m - 1)
-    forward(mats - 1)
-
-    for m in range(mats):
+    forward(len(chunks) - 1)
+
+    for m in range(len(chunks)):
         def held(od, _, m=m):
             unpack(2 * od + i, m)
             return 0
@@ -217,14 +231,16 @@
         def last(k, _, m=m):
             od = (o + k) % half
             d = 2 * od + (1 - i)
-            remote(gathered.at[d, m], gathered.at[d, m], sd.at[od, m], rc.at[d, m], mate).wait_recv()
+            remote(part(gathered, d, m), part(gathered, d, m), sd.at[od, m], rc.at[d, m], mate).wait_recv()
             unpack(d, m)
             return 0
 
         lax.fori_loop(0, half, last, 0)
-        working[m] = spread_out[...].astype(jnp.bfloat16)
-
-    for m in range(mats):
+        mat, lo, hi = chunks[m]
+        if hi == width:
+            working[mat] = spread_out[...].astype(jnp.bfloat16)
+
+    for m in range(len(chunks)):
         def given(k, _, m=m):
             copy_c(mate, k, m).wait_send()
             return 0
@@ -272,13 +288,13 @@
             pltpu.VMEM((3, mats, lines, width), jnp.float32),
             dma((n,)),
             dma((n,)),
-            dma((half, mats)),
-            dma((half, mats)),
-            dma((half, mats)),
-            dma((half, mats)),
-            dma((half, mats)),
-            dma((n, mats)),
-            dma((half, mats)),
+            dma((half, 2 * mats)),
+            dma((half, 2 * mats)),
+            dma((half, 2 * mats)),
+            dma((half, 2 * mats)),
+            dma((half, 2 * mats)),
+            dma((n, 2 * mats)),
+            dma((half, 2 * mats)),
         ],
         compiler_params=pltpu.CompilerParams(
             collective_id=0, has_side_effects=True, vmem_limit_bytes=60 * 2**20

time: 47.9 us -> 50.8 us (1.061)
  Pallas kernels: 40.7 us -> 43.6 us
    pallas_call x1, Pallas kernels: 40.7 us -> 43.6 us  [local(): pl.pallas_call(functools.partial(kernel, n, rows_dev, mats, pieces, width...]
where the time goes in v3:
time: 50.8 us; the launch traced here: 50.6 us
  Pallas kernels  43.6 us (86%)
  local copies, waits for them, and re-layouts  5.71 us (11%)
  between operations  1.3 us (3%)
    pallas_call x1, Pallas kernels, local(): pl.pallas_call(functools.partial(kernel, n, rows_dev, mats, pieces, width...  43.6 us
    unnamed x6, local copies, waits for them, and re-layouts  5.71 us

profile of v3, /device:TPU:0, one launch (start us, length us, event | category | flops | bytes accessed | tf_op | source)
XLA Modules:
  0.0 50.6 jit_solution(6250117986882320068)
XLA Ops:
  1.3 43.6 %shard_map.102 = (f32[3,2,7168]{2,1,0:T(2,128)}, f32[3,2,7168]{2,1,0:T(2,128)}, f32[3,2,7168]{2,1,0:T(2,128)}, bf16[3,16,7168]{2,1,0:T(8,128)(2,1)}) custom-call(f32[1,3,16,7168]{3,2,1,0:T(8,128)} %bitcast.8, s32[1,3]{1,0:T(1,128)} %counts_ref.1, s32[1]{0:T(128)S(6)} %copy.15.modality_ref, f32[3]{0:T(128)} %weight_ref.1, f32[3,2,7168]{2,1,0:T(2,128)} %bitcast.13, ...), custom_call_target="tpu_custom_call" | custom-call | tf_op jit(solution)/shard_map/pallas_call | solution.py:267
  44.9 0.0 copy-start
  44.9 1.7 %copy.16 = f32[2,3,7168]{2,0,1:T(2,128)} copy(f32[2,3,7168]{2,0,1:T(2,128)} %bitcast.12) | data formatting | bytes 344064
  46.5 1.6 %copy.17 = f32[2,3,7168]{2,0,1:T(2,128)} copy(f32[2,3,7168]{2,0,1:T(2,128)} %bitcast.11) | data formatting | bytes 344064
  48.1 1.6 %copy.18 = f32[2,3,7168]{2,0,1:T(2,128)} copy(f32[2,3,7168]{2,0,1:T(2,128)} %bitcast.10) | data formatting | bytes 344064
  49.7 0.0 copy-done
  49.7 0.8 %copy.19 = bf16[16,3,7168]{2,0,1:T(8,128)(2,1)} copy(bf16[16,3,7168]{2,0,1:T(8,128)(2,1)S(1)} %bitcast.9) | data formatting | bytes 1376256
Async XLA Ops:
  44.9 4.9 %copy-start = (bf16[3,16,7168]{2,1,0:T(8,128)(2,1)S(1)}, bf16[3,16,7168]{2,1,0:T(8,128)(2,1)}, u32[]{:S(2)}) copy-start(bf16[3,16,7168]{2,1,0:T(8,128)(2,1)} %get-tuple-element.11) | copy-start | bytes 2064388

commit v4 on v2

--- a/solution.py
+++ b/solution.py
@@ -105,6 +105,9 @@
             return 0
 
         lax.fori_loop(0, half, keep, 0)
+        pack(master_ref, state.at[0, m], 0, m)
+        pack(one_ref, state.at[1, m], 0, m)
+        pack(two_ref, state.at[2, m], 0, m)
 
     def hear(k, _):
         source = (me + k) % n
@@ -145,10 +148,6 @@
         return remote(gathered.at[me, m], gathered.at[me, m], sc.at[slot, m], rc.at[me, m], target)
 
     def finish(m):
-        pack(master_ref, state.at[0, m], 0, m)
-        pack(one_ref, state.at[1, m], 0, m)
-        pack(two_ref, state.at[2, m], 0, m)
-
         def add(k, total):
             source = (o + k) % half
             pltpu.make_async_remote_copy(
@@ -171,6 +170,8 @@
         state[0, m] = weights_new
         state[1, m] = first_new
         state[2, m] = second_new
+
+    def write_state(m):
         for slot, out in enumerate((master_out, one_out, two_out)):
             for r in range(rows_dev):
                 for p in range(pieces):
@@ -198,6 +199,23 @@
                 row = r * pieces + p
                 spread_out[pl.ds(d * rows_dev + r, 1), p * width : (p + 1) * width] = block[row : row + 1, :]
 
+    def collect(m):
+        def held(od, _):
+            unpack(2 * od + i, m)
+            return 0
+
+        lax.fori_loop(0, half, held, 0)
+
+        def last(k, _):
+            od = (o + k) % half
+            d = 2 * od + (1 - i)
+            remote(gathered.at[d, m], gathered.at[d, m], sd.at[od, m], rc.at[d, m], mate).wait_recv()
+            unpack(d, m)
+            return 0
+
+        lax.fori_loop(0, half, last, 0)
+        working[m] = spread_out[...].astype(jnp.bfloat16)
+
     phase_b(0)
     for m in range(mats):
         if m + 1 < mats:
@@ -206,23 +224,10 @@
         if m > 0:
             forward(m - 1)
     forward(mats - 1)
-
-    for m in range(mats):
-        def held(od, _, m=m):
-            unpack(2 * od + i, m)
-            return 0
-
-        lax.fori_loop(0, half, held, 0)
-
-        def last(k, _, m=m):
-            od = (o + k) % half
-            d = 2 * od + (1 - i)
-            remote(gathered.at[d, m], gathered.at[d, m], sd.at[od, m], rc.at[d, m], mate).wait_recv()
-            unpack(d, m)
-            return 0
-
-        lax.fori_loop(0, half, last, 0)
-        working[m] = spread_out[...].astype(jnp.bfloat16)
+    for m in range(mats):
+        write_state(m)
+    for m in range(mats):
+        collect(m)
 
     for m in range(mats):
         def given(k, _, m=m):

time: 47.9 us -> 47.9 us (level)
  no operation moved by 1% of the time
where the time goes in v4:
time: 47.9 us; the launch traced here: 47.7 us
  Pallas kernels  40.7 us (85%)
  local copies, waits for them, and re-layouts  5.71 us (12%)
  between operations  1.3 us (3%)
    pallas_call x1, Pallas kernels, local(): pl.pallas_call(functools.partial(kernel, n, rows_dev, mats, pieces, width...  40.7 us
    unnamed x6, local copies, waits for them, and re-layouts  5.71 us

profile of v4, /device:TPU:0, one launch (start us, length us, event | category | flops | bytes accessed | tf_op | source)
XLA Modules:
  0.0 47.7 jit_solution(15942759327986460238)
XLA Ops:
  1.3 40.7 %shard_map.102 = (f32[3,2,7168]{2,1,0:T(2,128)}, f32[3,2,7168]{2,1,0:T(2,128)}, f32[3,2,7168]{2,1,0:T(2,128)}, bf16[3,16,7168]{2,1,0:T(8,128)(2,1)}) custom-call(f32[1,3,16,7168]{3,2,1,0:T(8,128)} %bitcast.8, s32[1,3]{1,0:T(1,128)} %counts_ref.1, s32[1]{0:T(128)S(6)} %copy.15.modality_ref, f32[3]{0:T(128)} %weight_ref.1, f32[3,2,7168]{2,1,0:T(2,128)} %bitcast.13, ...), custom_call_target="tpu_custom_call" | custom-call | tf_op jit(solution)/shard_map/pallas_call | solution.py:256
  42.0 0.0 copy-start
  42.0 1.7 %copy.16 = f32[2,3,7168]{2,0,1:T(2,128)} copy(f32[2,3,7168]{2,0,1:T(2,128)} %bitcast.12) | data formatting | bytes 344064
  43.7 1.6 %copy.17 = f32[2,3,7168]{2,0,1:T(2,128)} copy(f32[2,3,7168]{2,0,1:T(2,128)} %bitcast.11) | data formatting | bytes 344064
  45.3 1.6 %copy.18 = f32[2,3,7168]{2,0,1:T(2,128)} copy(f32[2,3,7168]{2,0,1:T(2,128)} %bitcast.10) | data formatting | bytes 344064
  46.9 0.0 copy-done
  46.9 0.8 %copy.19 = bf16[16,3,7168]{2,0,1:T(8,128)(2,1)} copy(bf16[16,3,7168]{2,0,1:T(8,128)(2,1)S(1)} %bitcast.9) | data formatting | bytes 1376256
Async XLA Ops:
  42.0 4.9 %copy-start = (bf16[3,16,7168]{2,1,0:T(8,128)(2,1)S(1)}, bf16[3,16,7168]{2,1,0:T(8,128)(2,1)}, u32[]{:S(2)}) copy-start(bf16[3,16,7168]{2,1,0:T(8,128)(2,1)} %get-tuple-element.11) | copy-start | bytes 2064388

commit v5 on v4

--- a/solution.py
+++ b/solution.py
@@ -241,6 +241,19 @@
             return 0
 
         lax.fori_loop(1, half, sent, 0)
+
+
+def settle(count, mats, *refs):
+    sources, targets, sems = refs[:count], refs[count : 2 * count], refs[-1]
+    copies = [
+        pltpu.make_async_copy(source.at[m], target.at[m], sems.at[k, m])
+        for k, (source, target) in enumerate(zip(sources, targets))
+        for m in range(mats)
+    ]
+    for copy in copies:
+        copy.start()
+    for copy in copies:
+        copy.wait()
 
 
 def local(n, gradients, token_counts, modality, loss_weight, master, moment_one, moment_two):
@@ -292,7 +305,17 @@
         gradients.transpose(0, 2, 1, 3), token_counts, modality, loss_weight,
         master.transpose(1, 0, 2), moment_one.transpose(1, 0, 2), moment_two.transpose(1, 0, 2),
     )
-    return tuple(a.transpose(1, 0, 2) for a in (weights_new, first_new, second_new, working))
+    results = (weights_new, first_new, second_new, working)
+    count = len(results)
+    anywhere = pl.BlockSpec(memory_space=pl.ANY)
+    settled = pl.pallas_call(
+        functools.partial(settle, count, mats),
+        out_shape=tuple(jax.ShapeDtypeStruct(a.shape, a.dtype) for a in results),
+        in_specs=[anywhere] * count,
+        out_specs=(anywhere,) * count,
+        scratch_shapes=[dma((count, mats))],
+    )(*results)
+    return tuple(a.transpose(1, 0, 2) for a in settled)
 
 
 def solution(mesh):

time: 47.9 us -> 79.9 us (1.67)
  Pallas kernels: 40.7 us -> 78.4 us
  local copies, waits for them, and re-layouts: 5.71 us -> 0 us
    pallas_call x0 -> x1, Pallas kernels: none -> 37.7 us  [local(): pl.pallas_call(functools.partial(settle, count, mats), out_shape=tuple((j...]
    unnamed x6 -> x0, local copies, waits for them, and re-layouts: 5.71 us -> none
where the time goes in v5:
time: 79.9 us; the launch traced here: 79.7 us
  Pallas kernels  78.4 us (98%)
  between operations  1.29 us (2%)
    pallas_call x1, Pallas kernels, local(): pl.pallas_call(functools.partial(kernel, n, rows_dev, mats, pieces, width...  40.7 us
    pallas_call x1, Pallas kernels, local(): pl.pallas_call(functools.partial(settle, count, mats), out_shape=tuple((j...  37.7 us

profile of v5, /device:TPU:0, one launch (start us, length us, event | category | flops | bytes accessed | tf_op | source)
XLA Modules:
  0.0 79.7 jit_solution(14418088169114316481)
XLA Ops:
  1.3 40.7 %shard_map.102 = (f32[3,2,7168]{2,1,0:T(2,128)}, f32[3,2,7168]{2,1,0:T(2,128)}, f32[3,2,7168]{2,1,0:T(2,128)}, bf16[3,16,7168]{2,1,0:T(8,128)(2,1)}) custom-call(f32[1,3,16,7168]{3,2,1,0:T(8,128)} %bitcast.8, s32[1,3]{1,0:T(1,128)} %counts_ref.1, s32[1]{0:T(128)S(6)} %copy.11.modality_ref, f32[3]{0:T(128)} %weight_ref.1, f32[3,2,7168]{2,1,0:T(2,128)} %bitcast.9, ...), custom_call_target="tpu_custom_call" | custom-call | tf_op jit(solution)/shard_map/pallas_call | solution.py:269
  42.0 37.7 %shard_map.103 = (f32[3,2,7168]{2,1,0:T(2,128)}, f32[3,2,7168]{2,1,0:T(2,128)}, f32[3,2,7168]{2,1,0:T(2,128)}, bf16[3,16,7168]{2,1,0:T(8,128)(2,1)}) custom-call(f32[3,2,7168]{2,1,0:T(2,128)} %get-tuple-element.12.refs_0_, f32[3,2,7168]{2,1,0:T(2,128)} %get-tuple-element.13.refs_1_, f32[3,2,7168]{2,1,0:T(2,128)} %get-tuple-element.14.refs_2_, ...), custom_call_target="tpu_custom_call" | custom-call | tf_op jit(solution)/shard_map/pallas_call | solution.py:311

commit v6 on v4

--- a/solution.py
+++ b/solution.py
@@ -241,6 +241,12 @@
             return 0
 
         lax.fori_loop(1, half, sent, 0)
+
+
+def settle(count, mats, *refs):
+    for source, target in zip(refs[:count], refs[count:]):
+        for m in range(mats):
+            target[m] = source[m]
 
 
 def local(n, gradients, token_counts, modality, loss_weight, master, moment_one, moment_two):
@@ -292,7 +298,16 @@
         gradients.transpose(0, 2, 1, 3), token_counts, modality, loss_weight,
         master.transpose(1, 0, 2), moment_one.transpose(1, 0, 2), moment_two.transpose(1, 0, 2),
     )
-    return tuple(a.transpose(1, 0, 2) for a in (weights_new, first_new, second_new, working))
+    results = (weights_new, first_new, second_new, working)
+    count = len(results)
+    settled = pl.pallas_call(
+        functools.partial(settle, count, mats),
+        out_shape=tuple(jax.ShapeDtypeStruct(a.shape, a.dtype) for a in results),
+        in_specs=[vmem] * count,
+        out_specs=(vmem,) * count,
+        compiler_params=pltpu.CompilerParams(vmem_limit_bytes=60 * 2**20),
+    )(*results)
+    return tuple(a.transpose(1, 0, 2) for a in settled)
 
 
 def solution(mesh):

time: 47.9 us -> 44.6 us (0.931)
  local copies, waits for them, and re-layouts: 5.71 us -> 0 us
  Pallas kernels: 40.7 us -> 43.1 us
    unnamed x6 -> x0, local copies, waits for them, and re-layouts: 5.71 us -> none
    pallas_call x0 -> x1, Pallas kernels: none -> 2.39 us  [local(): pl.pallas_call(functools.partial(settle, count, mats), out_shape=tuple((j...]
where the time goes in v6:
time: 44.6 us; the launch traced here: 44.4 us
  Pallas kernels  43.1 us (97%)
  between operations  1.29 us (3%)
    pallas_call x1, Pallas kernels, local(): pl.pallas_call(functools.partial(kernel, n, rows_dev, mats, pieces, width...  40.7 us
    pallas_call x1, Pallas kernels, local(): pl.pallas_call(functools.partial(settle, count, mats), out_shape=tuple((j...  2.39 us

profile of v6, /device:TPU:0, one launch (start us, length us, event | category | flops | bytes accessed | tf_op | source)
XLA Modules:
  0.0 44.4 jit_solution(17483060245448936503)
XLA Ops:
  1.3 40.7 %shard_map.102 = (f32[3,2,7168]{2,1,0:T(2,128)}, f32[3,2,7168]{2,1,0:T(2,128)}, f32[3,2,7168]{2,1,0:T(2,128)}, bf16[3,16,7168]{2,1,0:T(8,128)(2,1)}) custom-call(f32[1,3,16,7168]{3,2,1,0:T(8,128)} %bitcast.8, s32[1,3]{1,0:T(1,128)} %counts_ref.1, s32[1]{0:T(128)S(6)} %copy.11.modality_ref, f32[3]{0:T(128)} %weight_ref.1, f32[3,2,7168]{2,1,0:T(2,128)} %bitcast.9, ...), custom_call_target="tpu_custom_call" | custom-call | tf_op jit(solution)/shard_map/pallas_call | solution.py:262
  42.0 2.4 %shard_map.103 = (f32[3,2,7168]{2,1,0:T(2,128)}, f32[3,2,7168]{2,1,0:T(2,128)}, f32[3,2,7168]{2,1,0:T(2,128)}, bf16[3,16,7168]{2,1,0:T(8,128)(2,1)}) custom-call(f32[3,2,7168]{2,1,0:T(2,128)} %get-tuple-element.12.refs_0_, f32[3,2,7168]{2,1,0:T(2,128)} %get-tuple-element.13.refs_1_, f32[3,2,7168]{2,1,0:T(2,128)} %get-tuple-element.14.refs_2_, ...), custom_call_target="tpu_custom_call" | custom-call | tf_op jit(solution)/shard_map/pallas_call | solution.py:303
